TPU v7x, 512 devices: a whole 4x4x16 slice. The times are simulated.
512 devices in a mesh: group: 8 (over z_lo), fsdp: 64 (over y, z_hi, x, core).
Axes of the slice: x: 4, y: 4, z: 16 (z_hi: 2, z_lo: 8; z = z_hi * 8 + z_lo), core: 2. Of those that a mesh axis runs over, the one named last changes fastest.
Arguments:
- outer_params: float32 [256, 28672], P('fsdp'), may hold values from -6 to 6
- outer_momentum: float32 [256, 28672], P('fsdp'), may hold values from -4 to 4
- first_moment: float32 [8, 256, 28672], P('group', 'fsdp'), may hold values from -0.0029296875 to 0.0029296875
- second_moment: float32 [8, 256, 28672], P('group', 'fsdp'), may hold values from 2.7247838e-08 to 2.724784e-07
- inner_grads: bfloat16 [8, 4, 256, 28672], P('group', None, 'fsdp'), may hold values from -120 to 120
Outputs:
- new_params: float32 [256, 28672], P('fsdp')
- new_momentum: float32 [256, 28672], P('fsdp')
All inputs are finite; a program needn't handle non-finite values.
Results may differ from a plain program's by a relative error of at most 0.0034.
Values may be sent and summed in bfloat16 or wider, within the bound.
No kernel may reach another device: no remote copies, remote signals or barrier semaphores. Data moves between devices by JAX's collectives and lax.ppermute only.
A program may use at most 64 MiB of HBM per device.

v0:
```python
import jax
import jax.numpy as jnp
from jax import lax
from jax.sharding import PartitionSpec as P

clip_norm = 1.0
beta_one = 0.9
beta_two = 0.95
inner_rate = 0.05
decay_rate = 0.1
epsilon = 1e-08
code_range = 448.0
outer_beta = 0.9
outer_rate = 0.7


def body(outer_params, outer_momentum, first_moment, second_moment, inner_grads):
    replicas = lax.axis_size("group")
    rows = outer_params.shape[0]
    width = outer_params.shape[1]
    grads = inner_grads[0]
    step_count = grads.shape[0]
    moment_one = first_moment[0]
    moment_two = second_moment[0]
    params = outer_params
    for step in range(step_count):
        grad = grads[step].astype(jnp.float32)
        total = lax.psum(jnp.sum(grad * grad), "fsdp")
        factor = jnp.minimum(1.0, clip_norm / (jnp.sqrt(total) + 1e-06))
        grad = grad * factor
        moment_one = beta_one * moment_one + (1.0 - beta_one) * grad
        moment_two = beta_two * moment_two + (1.0 - beta_two) * grad * grad
        params = params - inner_rate * (
            moment_one / (jnp.sqrt(moment_two) + epsilon) + decay_rate * params
        )
    blocks = (outer_params - params).reshape(rows, width // 128, 128)
    largest = jnp.max(jnp.abs(blocks), axis=-1)
    scales = (largest + 1e-06) / code_range
    codes = (blocks / scales[..., None]).astype(jnp.bfloat16).reshape(rows, width)
    all_codes, all_scales = (
        lax.all_gather(codes[None], "group", axis=0, tiled=True),
        lax.all_gather(scales[None].astype(jnp.bfloat16), "group", axis=0, tiled=True).astype(
            jnp.float32
        ),
    )
    decoded = (
        all_codes.astype(jnp.float32).reshape(replicas, rows, width // 128, 128)
        * all_scales[..., None]
    )
    average = (jnp.sum(decoded, axis=0) / replicas).reshape(rows, width)
    new_momentum = outer_beta * outer_momentum + average
    new_params = outer_params - outer_rate * (average + outer_beta * new_momentum)
    return (new_params, new_momentum)


def solution(mesh):
    return jax.shard_map(
        body,
        mesh=mesh,
        in_specs=(
            P("fsdp", None),
            P("fsdp", None),
            P("group", "fsdp", None),
            P("group", "fsdp", None),
            P("group", None, "fsdp", None),
        ),
        out_specs=(P("fsdp", None), P("fsdp", None)),
        check_vma=False,
    )
```

profile of v0, /device:TPU:6, one launch (start us, length us, event | category | flops | bytes accessed | tf_op | source)
XLA Modules:
  0.0 385.9 jit_solution(16076982088321555502)
XLA Ops:
  7.2 0.0 all-gather.6.cloned.1.call-start
  7.2 2.4 fusion.1
  9.7 252.7 %all-reduce = (f32[]{:T(128)}, f32[]{:T(128)}, f32[]{:T(128)}, f32[]{:T(128)}) all-reduce(f32[]{:T(128)} %get-tuple-element.4, f32[]{:T(128)} %get-tuple-element.5, f32[]{:T(128)} %get-tuple-element.3, f32[]{:T(128)} %get-tuple-element.2), channel_id=1, replica_groups=mesh['group'=8,'fsdp'=64] {'fsdp'}, use_global_device_ids=true, to_apply=%region_7.0 | all-reduce | flops 4 | bytes 32 | tf_op jit(solution)/shard_map/psum | solution.py:28
  265.3 4.2 %abs_bitcast_fusion = (f32[1,4,224,128]{3,1,2,0:T(4,128)S(1)}, f32[4,28672]{1,0:T(4,128)S(1)}) fusion(f32[4,28672]{1,0:T(4,128)} %param.5, f32[]{:T(128)S(6)} %min.15, bf16[1,4,4,28672]{3,2,1,0:T(4,128)(2,1)} %param.9, f32[]{:T(128)S(6)} %min.14, f32[]{:T(128)S(6)} %min.13, f32[1,4,28672]{2,1,0:T(4,128)} %param.8, f32[]{:T(128)S(6)} %min.12, ...), kind=kLoop, calls=%fused_computation.41 | loop fusion | flops 7110656 | bytes 3211280
  269.5 0.2 bitcast_reduce_fusion
  269.7 0.2 broadcast_bitcast_fusion
  269.9 1.0 fusion.25
  271.0 0.0 all-gather.6.cloned.1.call-update
  271.0 42.5 %all-gather.3 = bf16[8,4,224]{2,1,0:T(4,128)(2,1)S(1)} all-gather(bf16[1,4,224]{2,1,0:T(4,128)(2,1)S(1)} %get-tuple-element.15), channel_id=3, replica_groups=mesh['group'=8,'fsdp'=64] {'group'}, dimensions={0}, use_global_device_ids=true | all-gather | bytes 16128 | tf_op jit(solution)/shard_map/all_gather | solution.py:42
  313.5 2.4 mul.211
  315.9 5.2 %mul.212 = f32[8,4,28672]{2,1,0:T(4,128)} reshape(f32[8,4,224,128]{3,2,1,0:T(8,128)} %mul.211) | data formatting | bytes 7340032 | tf_op jit(solution)/shard_map/mul | solution.py:47
  321.1 0.0 copy-start
  321.1 0.0 copy-start.1
  321.1 52.9 %all-gather.6.cloned.1.call-done = bf16[8,4,28672]{2,1,0:T(4,128)(2,1)} async-done(((bf16[1,4,28672]{2,1,0:T(4,128)(2,1)}), bf16[8,4,28672]{2,1,0:T(4,128)(2,1)}) %all-gather.6.cloned.1.call-update) | async-done | bytes 1835024 | tf_op jit(solution)/shard_map/all_gather | solution.py:41
  374.0 3.8 fusion
  377.8 0.0 copy-done
  377.8 0.0 copy-done.1
  377.8 1.3 multiply_subtract_fusion
  (1 shorter events, 0.0 us)
Async XLA Ops:
  7.2 366.8 %all-gather.6.cloned.1.call-start = ((), (), s32[]{:S(2)}) async-start(), calls=%async_computation | async-start | bytes 2064384 | tf_op jit(solution)/shard_map/all_gather | solution.py:41
  321.1 56.7 %copy-start = (f32[4,28672]{1,0:T(4,128)S(1)}, f32[4,28672]{1,0:T(4,128)}, u32[]{:S(2)}) copy-start(f32[4,28672]{1,0:T(4,128)} %param.5) | copy-start | bytes 1376260
  321.1 56.7 %copy-start.1 = (f32[4,28672]{1,0:T(4,128)S(1)}, f32[4,28672]{1,0:T(4,128)}, u32[]{:S(2)}) copy-start(f32[4,28672]{1,0:T(4,128)} %param.6) | copy-start | bytes 1376260
Sparse Core Ops, SparseCore 0:
  271.1 102.8 all-gather.5
where the time goes:
time: 387 us; the launch traced here: 386 us
  blocking collectives  295 us (76%)
  waiting for transfers between devices  52.9 us (14%)
  between operations  17 us (4%)
  other arithmetic  13 us (3%)
  local copies, waits for them, and re-layouts  7.76 us (2%)
    psum x1, blocking collectives, body(): total = lax.psum(jnp.sum(grad * grad), 'fsdp')  253 us
    all_gather x1, waiting for transfers between devices, body(): lax.all_gather(codes[None], 'group', axis=0, tiled=True)  52.9 us
    all_gather x1, blocking collectives, body(): lax.all_gather(scales[None].astype(jnp.bfloat16), 'group', axis=0, tiled=...  42.5 us
  transfers between devices with their start and end apart: 1, of which 1 were waited for; matrix products, arithmetic and copies ran while one was open for 2% of the time, Pallas kernels for 0%

commit v1 on v0

v1 whole, which is shorter than its diff:
```python
import jax
import jax.numpy as jnp
from jax import lax
from jax.experimental import pallas as pl
from jax.experimental.pallas import tpu as pltpu
from jax.sharding import PartitionSpec as P

clip_norm = 1.0
beta_one = 0.9
beta_two = 0.95
inner_rate = 0.05
decay_rate = 0.1
epsilon = 1e-08
outer_beta = 0.9
outer_rate = 0.7
sent = jnp.bfloat16


def to_rows(x):
    lead = x.shape[:-2]
    rows, width = x.shape[-2:]
    x = x.reshape(lead + (rows, width // 128, 128))
    x = jnp.swapaxes(x, -3, -2)
    return x.reshape(lead + (rows * width // 128, 128))


def from_rows(x, rows, width):
    return jnp.swapaxes(x.reshape(width // 128, rows, 128), 0, 1).reshape(rows, width)


def squares_kernel(grads_ref, out_ref):
    steps, length, _ = grads_ref.shape
    lane = lax.broadcasted_iota(jnp.int32, (1, 128), 1)
    row = jnp.zeros((1, 128), jnp.float32)
    for step in range(steps):
        total = jnp.zeros((16, 128), jnp.float32)
        for at in range(0, length, 16):
            grad = grads_ref[step, at : at + 16, :].astype(jnp.float32)
            total = total + grad * grad
        row = jnp.where(lane == step, jnp.sum(total), row)
    out_ref[...] = jnp.broadcast_to(row, out_ref.shape)


def inner_kernel(totals_ref, params_ref, one_ref, two_ref, grads_ref, out_ref):
    steps, length, _ = grads_ref.shape
    totals = jnp.sum(totals_ref[...], axis=0, keepdims=True)
    factors = jnp.minimum(1.0, clip_norm / (jnp.sqrt(totals) + 1e-06))
    lane = lax.broadcasted_iota(jnp.int32, (1, 128), 1)
    factor = [jnp.sum(jnp.where(lane == step, factors, 0.0)) for step in range(steps)]
    for at in range(0, length, 16):
        rows = slice(at, at + 16)
        start = params_ref[rows, :]
        params = start
        moment_one = one_ref[rows, :]
        moment_two = two_ref[rows, :]
        for step in range(steps):
            grad = grads_ref[step, rows, :].astype(jnp.float32) * factor[step]
            moment_one = beta_one * moment_one + (1.0 - beta_one) * grad
            moment_two = beta_two * moment_two + (1.0 - beta_two) * grad * grad
            params = params - inner_rate * (
                moment_one / (jnp.sqrt(moment_two) + epsilon) + decay_rate * params
            )
        out_ref[rows, :] = (start - params).astype(out_ref.dtype)


def mean_kernel(in_ref, out_ref):
    replicas, length, _ = in_ref.shape
    for at in range(0, length, 16):
        rows = slice(at, at + 16)
        total = in_ref[0, rows, :].astype(jnp.float32)
        for group in range(1, replicas):
            total = total + in_ref[group, rows, :].astype(jnp.float32)
        total = (total / replicas).astype(out_ref.dtype)
        for group in range(replicas):
            out_ref[group, rows, :] = total


def outer_kernel(average_ref, params_ref, momentum_ref, new_params_ref, new_momentum_ref):
    length = average_ref.shape[0]
    for at in range(0, length, 16):
        rows = slice(at, at + 16)
        average = average_ref[rows, :].astype(jnp.float32)
        momentum = outer_beta * momentum_ref[rows, :] + average
        new_momentum_ref[rows, :] = momentum
        new_params_ref[rows, :] = params_ref[rows, :] - outer_rate * (
            average + outer_beta * momentum
        )


def call(kernel, out_shape, *args):
    return pl.pallas_call(
        kernel,
        out_shape=out_shape,
        compiler_params=pltpu.CompilerParams(vmem_limit_bytes=16 * 1024 * 1024),
    )(*args)


def body(outer_params, outer_momentum, first_moment, second_moment, inner_grads):
    replicas = lax.axis_size("group")
    shards = lax.axis_size("fsdp")
    rows, width = outer_params.shape
    length = rows * width // 128
    params = to_rows(outer_params)
    momentum = to_rows(outer_momentum)
    moment_one = to_rows(first_moment[0])
    moment_two = to_rows(second_moment[0])
    grads = to_rows(inner_grads[0])
    f32 = jnp.float32
    squares = call(squares_kernel, jax.ShapeDtypeStruct((shards, 128), f32), grads)
    totals = lax.all_to_all(squares, "fsdp", 0, 0, tiled=True)
    delta = call(
        inner_kernel,
        jax.ShapeDtypeStruct((length, 128), sent),
        totals,
        params,
        moment_one,
        moment_two,
        grads,
    )
    delta = delta.reshape(replicas, length // replicas, 128)
    parts = lax.all_to_all(delta, "group", 0, 0, tiled=True)
    mean = call(mean_kernel, jax.ShapeDtypeStruct(parts.shape, sent), parts)
    average = lax.all_to_all(mean, "group", 0, 0, tiled=True).reshape(length, 128)
    out = jax.ShapeDtypeStruct((length, 128), f32)
    new_params, new_momentum = call(outer_kernel, (out, out), average, params, momentum)
    return (from_rows(new_params, rows, width), from_rows(new_momentum, rows, width))


def solution(mesh):
    return jax.shard_map(
        body,
        mesh=mesh,
        in_specs=(
            P("fsdp", None),
            P("fsdp", None),
            P("group", "fsdp", None),
            P("group", "fsdp", None),
            P("group", None, "fsdp", None),
        ),
        out_specs=(P("fsdp", None), P("fsdp", None)),
        check_vma=False,
    )
```

time: 387 us -> 83.6 us (0.22)
  the two profiles are of different devices: /device:TPU:6 before, /device:TPU:32 now
where the time goes in v1:
time: 83.6 us; the launch traced here: 83.3 us
  blocking collectives  77.6 us (93%)
  Pallas kernels  2.76 us (3%)
  local copies, waits for them, and re-layouts  2.2 us (3%)
    all_to_all x1, blocking collectives, body(): totals = lax.all_to_all(squares, 'fsdp', 0, 0, tiled=True)  36.9 us
    all_to_all x1, blocking collectives, body(): parts = lax.all_to_all(delta, 'group', 0, 0, tiled=True)  20.8 us
    all_to_all x1, blocking collectives, body(): lax.all_to_all(mean, 'group', 0, 0, tiled=True).reshape(length, 128)  20 us
    pallas_call x4, Pallas kernels, call(): pl.pallas_call(kernel, out_shape=out_shape, compiler_params=pltpu.Compile...  2.76 us
    unnamed x10, local copies, waits for them, and re-layouts  2.2 us

profile of v1, /device:TPU:32, one launch (start us, length us, event | category | flops | bytes accessed | tf_op | source)
XLA Modules:
  0.0 83.3 jit_solution(5448001835989872479)
XLA Ops:
  0.6 0.0 copy-start
  0.6 1.2 %copy-done = bf16[1,4,4,28672]{3,2,1,0:T(4,128)(2,1)S(1)} copy-done((bf16[1,4,4,28672]{3,2,1,0:T(4,128)(2,1)S(1)}, bf16[1,4,4,28672]{3,2,1,0:T(4,128)(2,1)}, u32[]{:S(2)}) %copy-start) | copy-done | bytes 917528
  1.8 0.0 copy-start.1
  1.8 0.0 copy-start.2
  1.8 0.2 shard_map.68
  2.0 36.9 %all_to_all.21 = f32[64,1,128]{2,1,0:T(1,128)S(1)} all-to-all(f32[64,1,128]{2,1,0:T(1,128)S(1)} %bitcast.51), channel_id=1, replica_groups=mesh['group'=8,'fsdp'=64] {'fsdp'}, dimensions={0} | all-to-all | bytes 65536 | tf_op jit(solution)/shard_map/all_to_all | solution.py:110
  38.9 0.0 copy-done.1
  38.9 0.0 copy-done.2
  38.9 0.0 copy-start.3
  38.9 1.0 %copy-done.3 = f32[1,4,28672]{2,1,0:T(4,128)S(1)} copy-done((f32[1,4,28672]{2,1,0:T(4,128)S(1)}, f32[1,4,28672]{2,1,0:T(4,128)}, u32[]{:S(2)}) %copy-start.3) | copy-done | bytes 458776
  39.9 1.5 %shard_map.69 = bf16[896,128]{1,0:T(8,128)(2,1)S(1)} custom-call(f32[64,128]{1,0:T(8,128)S(1)} %bitcast.50, f32[896,128]{1,0:T(8,128)S(1)} %bitcast.43, f32[896,128]{1,0:T(8,128)S(1)} %bitcast.47, f32[896,128]{1,0:T(8,128)S(1)} %bitcast.48, bf16[4,896,128]{2,1,0:T(8,128)(2,1)S(1)} %bitcast.42), custom_call_target="tpu_custom_call" | custom-call | tf_op jit(solution)/shard_map/pallas_call | solution.py:91
  41.5 20.8 %all_to_all.22.in_ref = bf16[8,112,128]{2,1,0:T(8,128)(2,1)S(1)} all-to-all(bf16[8,112,128]{2,1,0:T(8,128)(2,1)S(1)} %bitcast.45), channel_id=1, replica_groups=mesh['group'=8,'fsdp'=64] {'group'}, dimensions={0} | all-to-all | bytes 458752 | tf_op jit(solution)/shard_map/all_to_all | solution.py:121
  62.2 0.0 copy-start.4
  62.3 20.0 %all_to_all.23 = bf16[8,112,128]{2,1,0:T(8,128)(2,1)S(1)} all-to-all(bf16[8,112,128]{2,1,0:T(8,128)(2,1)S(1)} %shard_map.70), channel_id=1, replica_groups=mesh['group'=8,'fsdp'=64] {'group'}, dimensions={0} | all-to-all | bytes 458752 | tf_op jit(solution)/shard_map/all_to_all | solution.py:123
  82.2 0.0 copy-done.4
  82.2 1.0 %shard_map.71 = (f32[896,128]{1,0:T(8,128)}, f32[896,128]{1,0:T(8,128)}) custom-call(bf16[896,128]{1,0:T(8,128)(2,1)S(1)} %bitcast.46, f32[896,128]{1,0:T(8,128)S(1)} %bitcast.44, f32[896,128]{1,0:T(8,128)S(1)} %bitcast.49), custom_call_target="tpu_custom_call" | custom-call | tf_op jit(solution)/shard_map/pallas_call | solution.py:91
  (1 shorter events, 0.0 us)
Async XLA Ops:
  0.6 1.2 %copy-start = (bf16[1,4,4,28672]{3,2,1,0:T(4,128)(2,1)S(1)}, bf16[1,4,4,28672]{3,2,1,0:T(4,128)(2,1)}, u32[]{:S(2)}) copy-start(bf16[1,4,4,28672]{3,2,1,0:T(4,128)(2,1)} %param.9) | copy-start | bytes 2752516
  1.8 37.1 %copy-start.1 = (f32[4,28672]{1,0:T(4,128)S(1)}, f32[4,28672]{1,0:T(4,128)}, u32[]{:S(2)}) copy-start(f32[4,28672]{1,0:T(4,128)} %param.5) | copy-start | bytes 1376260
  1.8 37.1 %copy-start.2 = (f32[1,4,28672]{2,1,0:T(4,128)S(1)}, f32[1,4,28672]{2,1,0:T(4,128)}, u32[]{:S(2)}) copy-start(f32[1,4,28672]{2,1,0:T(4,128)} %param.7) | copy-start | bytes 1376260
  38.9 1.0 %copy-start.3 = (f32[1,4,28672]{2,1,0:T(4,128)S(1)}, f32[1,4,28672]{2,1,0:T(4,128)}, u32[]{:S(2)}) copy-start(f32[1,4,28672]{2,1,0:T(4,128)} %param.8) | copy-start | bytes 1376260
  62.2 20.0 %copy-start.4 = (f32[4,28672]{1,0:T(4,128)S(1)}, f32[4,28672]{1,0:T(4,128)}, u32[]{:S(2)}) copy-start(f32[4,28672]{1,0:T(4,128)} %param.6) | copy-start | bytes 1376260

commit v2 on v1

--- a/solution.py
+++ b/solution.py
@@ -14,6 +14,10 @@
 outer_beta = 0.9
 outer_rate = 0.7
 sent = jnp.bfloat16
+
+line_order = [4, 5, 6, 7, 3, 2, 1, 0]
+totals_first = ((2 * 2 + 1) * 4 + 2) * 2
+totals_order = [totals_first] + [k for k in range(64) if k != totals_first]
 
 
 def to_rows(x):
@@ -107,7 +111,7 @@
     grads = to_rows(inner_grads[0])
     f32 = jnp.float32
     squares = call(squares_kernel, jax.ShapeDtypeStruct((shards, 128), f32), grads)
-    totals = lax.all_to_all(squares, "fsdp", 0, 0, tiled=True)
+    totals = lax.all_to_all(squares, "fsdp", 0, 0, tiled=True, axis_index_groups=[totals_order])
     delta = call(
         inner_kernel,
         jax.ShapeDtypeStruct((length, 128), sent),
@@ -118,9 +122,10 @@
         grads,
     )
     delta = delta.reshape(replicas, length // replicas, 128)
-    parts = lax.all_to_all(delta, "group", 0, 0, tiled=True)
+    parts = lax.all_to_all(delta, "group", 0, 0, tiled=True, axis_index_groups=[line_order])
     mean = call(mean_kernel, jax.ShapeDtypeStruct(parts.shape, sent), parts)
-    average = lax.all_to_all(mean, "group", 0, 0, tiled=True).reshape(length, 128)
+    average = lax.all_to_all(mean, "group", 0, 0, tiled=True, axis_index_groups=[line_order])
+    average = average.reshape(length, 128)
     out = jax.ShapeDtypeStruct((length, 128), f32)
     new_params, new_momentum = call(outer_kernel, (out, out), average, params, momentum)
     return (from_rows(new_params, rows, width), from_rows(new_momentum, rows, width))

time: 83.6 us -> 65.9 us (0.79)
  the two profiles are of different devices: /device:TPU:32 before, /device:TPU:6 now
where the time goes in v2:
time: 65.9 us; the launch traced here: 65.6 us
  blocking collectives  60 us (91%)
  Pallas kernels  2.76 us (4%)
  local copies, waits for them, and re-layouts  2.2 us (3%)
  between operations  0.66 us (1%)
    all_to_all x1, blocking collectives, body(): lax.all_to_all(squares, 'fsdp', 0, 0, tiled=True, axis_index_groups=[tota...  25 us
    all_to_all x1, blocking collectives, body(): lax.all_to_all(delta, 'group', 0, 0, tiled=True, axis_index_groups=[line_...  19.6 us
    all_to_all x1, blocking collectives, body(): lax.all_to_all(mean, 'group', 0, 0, tiled=True, axis_index_groups=[line_o...  15.4 us
    pallas_call x4, Pallas kernels, call(): pl.pallas_call(kernel, out_shape=out_shape, compiler_params=pltpu.Compile...  2.76 us
    unnamed x10, local copies, waits for them, and re-layouts  2.2 us

profile of v2, /device:TPU:6, one launch (start us, length us, event | category | flops | bytes accessed | tf_op | source)
XLA Modules:
  0.0 65.6 jit_solution(3063245111165039050)
XLA Ops:
  0.6 0.0 copy-start
  0.6 1.2 %copy-done = bf16[1,4,4,28672]{3,2,1,0:T(4,128)(2,1)S(1)} copy-done((bf16[1,4,4,28672]{3,2,1,0:T(4,128)(2,1)S(1)}, bf16[1,4,4,28672]{3,2,1,0:T(4,128)(2,1)}, u32[]{:S(2)}) %copy-start) | copy-done | bytes 917528
  1.8 0.0 copy-start.1
  1.8 0.0 copy-start.2
  1.8 0.2 shard_map.68
  2.0 25.0 %all_to_all.21 = f32[64,1,128]{2,1,0:T(1,128)S(1)} all-to-all(f32[64,1,128]{2,1,0:T(1,128)S(1)} %bitcast.51), channel_id=1, replica_groups={{44,0,1,2,3,4,5,6,7,8,9,10,11,12,13,14,15,16,17,18,19,20,21,22,23,24,25..., dimensions={0} | all-to-all | bytes 65536 | tf_op jit(solution)/shard_map/all_to_all | solution.py:114
  27.0 0.0 copy-done.1
  27.0 0.0 copy-done.2
  27.0 0.0 copy-start.3
  27.0 1.0 %copy-done.3 = f32[1,4,28672]{2,1,0:T(4,128)S(1)} copy-done((f32[1,4,28672]{2,1,0:T(4,128)S(1)}, f32[1,4,28672]{2,1,0:T(4,128)}, u32[]{:S(2)}) %copy-start.3) | copy-done | bytes 458776
  28.0 1.5 %shard_map.69 = bf16[896,128]{1,0:T(8,128)(2,1)S(1)} custom-call(f32[64,128]{1,0:T(8,128)S(1)} %bitcast.50, f32[896,128]{1,0:T(8,128)S(1)} %bitcast.43, f32[896,128]{1,0:T(8,128)S(1)} %bitcast.47, f32[896,128]{1,0:T(8,128)S(1)} %bitcast.48, bf16[4,896,128]{2,1,0:T(8,128)(2,1)S(1)} %bitcast.42), custom_call_target="tpu_custom_call" | custom-call | tf_op jit(solution)/shard_map/pallas_call | solution.py:95
  29.5 19.6 %all_to_all.22.in_ref = bf16[8,112,128]{2,1,0:T(8,128)(2,1)S(1)} all-to-all(bf16[8,112,128]{2,1,0:T(8,128)(2,1)S(1)} %bitcast.45), channel_id=1, replica_groups={{256,320,384,448,192,128,64,0},{257,321,385,449,193,129,65,1},{258,322,..., dimensions={0} | all-to-all | bytes 458752 | tf_op jit(solution)/shard_map/all_to_all | solution.py:125
  49.1 0.0 copy-start.4
  49.2 15.4 %all_to_all.23 = bf16[8,112,128]{2,1,0:T(8,128)(2,1)S(1)} all-to-all(bf16[8,112,128]{2,1,0:T(8,128)(2,1)S(1)} %shard_map.70), channel_id=1, replica_groups={{256,320,384,448,192,128,64,0},{257,321,385,449,193,129,65,1},{258,322,..., dimensions={0} | all-to-all | bytes 458752 | tf_op jit(solution)/shard_map/all_to_all | solution.py:127
  64.6 0.0 copy-done.4
  64.6 1.0 %shard_map.71 = (f32[896,128]{1,0:T(8,128)}, f32[896,128]{1,0:T(8,128)}) custom-call(bf16[896,128]{1,0:T(8,128)(2,1)S(1)} %bitcast.46, f32[896,128]{1,0:T(8,128)S(1)} %bitcast.44, f32[896,128]{1,0:T(8,128)S(1)} %bitcast.49), custom_call_target="tpu_custom_call" | custom-call | tf_op jit(solution)/shard_map/pallas_call | solution.py:95
  (1 shorter events, 0.0 us)
Async XLA Ops:
  0.6 1.2 %copy-start = (bf16[1,4,4,28672]{3,2,1,0:T(4,128)(2,1)S(1)}, bf16[1,4,4,28672]{3,2,1,0:T(4,128)(2,1)}, u32[]{:S(2)}) copy-start(bf16[1,4,4,28672]{3,2,1,0:T(4,128)(2,1)} %param.9) | copy-start | bytes 2752516
  1.8 25.1 %copy-start.1 = (f32[4,28672]{1,0:T(4,128)S(1)}, f32[4,28672]{1,0:T(4,128)}, u32[]{:S(2)}) copy-start(f32[4,28672]{1,0:T(4,128)} %param.5) | copy-start | bytes 1376260
  1.8 25.1 %copy-start.2 = (f32[1,4,28672]{2,1,0:T(4,128)S(1)}, f32[1,4,28672]{2,1,0:T(4,128)}, u32[]{:S(2)}) copy-start(f32[1,4,28672]{2,1,0:T(4,128)} %param.7) | copy-start | bytes 1376260
  27.0 1.0 %copy-start.3 = (f32[1,4,28672]{2,1,0:T(4,128)S(1)}, f32[1,4,28672]{2,1,0:T(4,128)}, u32[]{:S(2)}) copy-start(f32[1,4,28672]{2,1,0:T(4,128)} %param.8) | copy-start | bytes 1376260
  49.1 15.5 %copy-start.4 = (f32[4,28672]{1,0:T(4,128)S(1)}, f32[4,28672]{1,0:T(4,128)}, u32[]{:S(2)}) copy-start(f32[4,28672]{1,0:T(4,128)} %param.6) | copy-start | bytes 1376260

commit v3 on v2

v3 whole, which is shorter than its diff:
```python
import jax
import jax.numpy as jnp
from jax import lax
from jax.experimental import pallas as pl
from jax.experimental.pallas import tpu as pltpu
from jax.sharding import PartitionSpec as P

clip_norm = 1.0
beta_one = 0.9
beta_two = 0.95
inner_rate = 0.05
decay_rate = 0.1
epsilon = 1e-08
outer_beta = 0.9
outer_rate = 0.7
sent = jnp.bfloat16

codes_order = [4, 6, 7, 0, 1, 5, 3, 2]
means_order = [4, 6, 1, 2, 5, 3, 0, 7]
totals_first = ((2 * 2 + 1) * 4 + 2) * 2
totals_order = [totals_first] + [k for k in range(64) if k != totals_first]


def to_rows(x):
    lead = x.shape[:-2]
    rows, width = x.shape[-2:]
    x = x.reshape(lead + (rows, width // 128, 128))
    x = jnp.swapaxes(x, -3, -2)
    return x.reshape(lead + (rows * width // 128, 128))


def from_rows(x, rows, width):
    return jnp.swapaxes(x.reshape(width // 128, rows, 128), 0, 1).reshape(rows, width)


def squares_kernel(*refs):
    grads_refs, out_ref = refs[:-1], refs[-1]
    steps, (length, _) = len(grads_refs), grads_refs[0].shape
    lane = lax.broadcasted_iota(jnp.int32, (1, 128), 1)
    row = jnp.zeros((1, 128), jnp.float32)
    for step in range(steps):
        total = jnp.zeros((16, 128), jnp.float32)
        for at in range(0, length, 16):
            grad = grads_refs[step][at : at + 16, :].astype(jnp.float32)
            total = total + grad * grad
        row = jnp.where(lane == step, jnp.sum(total), row)
    out_ref[...] = jnp.broadcast_to(row, out_ref.shape)


def inner_kernel(totals_ref, params_ref, one_ref, two_ref, *refs):
    grads_refs, out_ref = refs[:-1], refs[-1]
    steps, (length, _) = len(grads_refs), grads_refs[0].shape
    totals = jnp.sum(totals_ref[...], axis=0, keepdims=True)
    factors = jnp.minimum(1.0, clip_norm / (jnp.sqrt(totals) + 1e-06))
    lane = lax.broadcasted_iota(jnp.int32, (1, 128), 1)
    kept = (1.0 - inner_rate * decay_rate) ** steps
    adds_one, adds_two, terms, weights = [], [], [], []
    for step in range(steps):
        factor = jnp.sum(jnp.where(lane == step, factors, 0.0))
        shrunk_one = beta_one ** (step + 1)
        shrunk_two = beta_two ** (step + 1)
        left = (1.0 - inner_rate * decay_rate) ** (steps - 1 - step)
        adds_one.append(factor * ((1.0 - beta_one) / shrunk_one))
        adds_two.append(factor * factor * ((1.0 - beta_two) / shrunk_two))
        terms.append(epsilon / shrunk_two**0.5)
        weights.append(inner_rate * left * shrunk_one / shrunk_two**0.5)
    for at in range(0, length, 16):
        rows = slice(at, at + 16)
        delta = (1.0 - kept) * params_ref[rows, :]
        moment_one = one_ref[rows, :]
        moment_two = two_ref[rows, :]
        for step in range(steps):
            grad = grads_refs[step][rows, :].astype(jnp.float32)
            moment_one = moment_one + adds_one[step] * grad
            moment_two = moment_two + adds_two[step] * (grad * grad)
            root = moment_two * lax.rsqrt(moment_two) + terms[step]
            delta = delta + (weights[step] * moment_one) / root
        out_ref[rows, :] = delta.astype(out_ref.dtype)


def mean_kernel(in_ref, out_ref):
    replicas, length, _ = in_ref.shape
    for at in range(0, length, 16):
        rows = slice(at, at + 16)
        total = in_ref[0, rows, :].astype(jnp.float32)
        for group in range(1, replicas):
            total = total + in_ref[group, rows, :].astype(jnp.float32)
        total = (total / replicas).astype(out_ref.dtype)
        for group in range(replicas):
            out_ref[group, rows, :] = total


def outer_kernel(average_ref, params_ref, momentum_ref, new_params_ref, new_momentum_ref):
    _, length, _ = average_ref.shape
    for part, owner in enumerate(codes_order):
        slot = means_order.index(owner)
        for at in range(0, length, 16):
            rows = slice(part * length + at, part * length + at + 16)
            average = average_ref[slot, at : at + 16, :].astype(jnp.float32)
            momentum = outer_beta * momentum_ref[rows, :] + average
            new_momentum_ref[rows, :] = momentum
            new_params_ref[rows, :] = params_ref[rows, :] - outer_rate * (
                average + outer_beta * momentum
            )


def call(kernel, out_shape, *args):
    return pl.pallas_call(
        kernel,
        out_shape=out_shape,
        compiler_params=pltpu.CompilerParams(vmem_limit_bytes=16 * 1024 * 1024),
    )(*args)


def body(outer_params, outer_momentum, first_moment, second_moment, inner_grads):
    replicas = lax.axis_size("group")
    shards = lax.axis_size("fsdp")
    rows, width = outer_params.shape
    length = rows * width // 128
    params = to_rows(outer_params)
    momentum = to_rows(outer_momentum)
    moment_one = to_rows(first_moment[0])
    moment_two = to_rows(second_moment[0])
    grads = [to_rows(inner_grads[0, step]) for step in range(inner_grads.shape[1])]
    f32 = jnp.float32
    squares = call(squares_kernel, jax.ShapeDtypeStruct((shards, 128), f32), *grads)
    totals = lax.all_to_all(squares, "fsdp", 0, 0, tiled=True, axis_index_groups=[totals_order])
    delta = call(
        inner_kernel,
        jax.ShapeDtypeStruct((length, 128), sent),
        totals,
        params,
        moment_one,
        moment_two,
        *grads,
    )
    delta = delta.reshape(replicas, length // replicas, 128)
    parts = lax.all_to_all(delta, "group", 0, 0, tiled=True, axis_index_groups=[codes_order])
    mean = call(mean_kernel, jax.ShapeDtypeStruct(parts.shape, sent), parts)
    average = lax.all_to_all(mean, "group", 0, 0, tiled=True, axis_index_groups=[means_order])
    out = jax.ShapeDtypeStruct((length, 128), f32)
    new_params, new_momentum = call(outer_kernel, (out, out), average, params, momentum)
    return (from_rows(new_params, rows, width), from_rows(new_momentum, rows, width))


def solution(mesh):
    return jax.shard_map(
        body,
        mesh=mesh,
        in_specs=(
            P("fsdp", None),
            P("fsdp", None),
            P("group", "fsdp", None),
            P("group", "fsdp", None),
            P("group", None, "fsdp", None),
        ),
        out_specs=(P("fsdp", None), P("fsdp", None)),
        check_vma=False,
    )
```

time: 65.9 us -> 63.6 us (0.965)
  blocking collectives: 60 us -> 58.9 us
    unnamed x10 -> x8, local copies, waits for them, and re-layouts: 2.2 us -> 0.02 us
    slice x0 -> x1, local copies, waits for them, and re-layouts: none -> 1.64 us  [body(): inner_grads[0, step]]
    all_to_all x2, blocking collectives: 35 us -> 33.9 us  [the longest x1 19.6 us: body(): lax.all_to_all(delta, 'group', 0, 0, tiled=True, axis_index_groups=[codes...]
where the time goes in v3:
time: 63.6 us; the launch traced here: 63.4 us
  blocking collectives  58.9 us (93%)
  Pallas kernels  2.17 us (3%)
  local copies, waits for them, and re-layouts  1.66 us (3%)
  between operations  0.68 us (1%)
    all_to_all x1, blocking collectives, body(): lax.all_to_all(squares, 'fsdp', 0, 0, tiled=True, axis_index_groups=[tota...  25 us
    all_to_all x1, blocking collectives, body(): lax.all_to_all(delta, 'group', 0, 0, tiled=True, axis_index_groups=[codes...  19.6 us
    all_to_all x1, blocking collectives, body(): lax.all_to_all(mean, 'group', 0, 0, tiled=True, axis_index_groups=[means_...  14.4 us
    pallas_call x4, Pallas kernels, call(): pl.pallas_call(kernel, out_shape=out_shape, compiler_params=pltpu.Compile...  2.17 us
    slice x1, local copies, waits for them, and re-layouts, body(): inner_grads[0, step]  1.64 us

profile of v3, /device:TPU:6, one launch (start us, length us, event | category | flops | bytes accessed | tf_op | source)
XLA Modules:
  0.0 63.4 jit_solution(16786731891967326180)
XLA Ops:
  0.6 0.0 copy-start.2
  0.6 1.6 %fusion = (bf16[1,1,4,28672]{3,2,1,0:T(4,128)(2,1)S(1)}, bf16[1,1,4,28672]{3,2,1,0:T(4,128)(2,1)S(1)}, bf16[1,1,4,28672]{3,2,1,0:T(4,128)(2,1)S(1)}, bf16[1,1,4,28672]{3,2,1,0:T(4,128)(2,1)S(1)}) fusion(bf16[1,4,4,28672]{3,2,1,0:T(4,128)(2,1)} %param.9), kind=kLoop, calls=%fused_computation | loop fusion | bytes 1835008 | tf_op jit(solution)/shard_map/slice | solution.py:124
  2.3 0.0 copy-start
  2.3 0.0 copy-start.1
  2.3 0.2 shard_map.68
  2.5 25.0 %all_to_all.21 = f32[64,1,128]{2,1,0:T(1,128)S(1)} all-to-all(f32[64,1,128]{2,1,0:T(1,128)S(1)} %bitcast.70), channel_id=1, replica_groups={{44,0,1,2,3,4,5,6,7,8,9,10,11,12,13,14,15,16,17,18,19,20,21,22,23,24,25..., dimensions={0} | all-to-all | bytes 65536 | tf_op jit(solution)/shard_map/all_to_all | solution.py:127
  27.4 0.0 copy-done.2
  27.5 0.0 copy-done
  27.5 0.0 copy-done.1
  27.5 0.9 %shard_map.69 = bf16[896,128]{1,0:T(8,128)(2,1)S(1)} custom-call(f32[64,128]{1,0:T(8,128)S(1)} %bitcast.69, f32[896,128]{1,0:T(8,128)S(1)} %bitcast.63, f32[896,128]{1,0:T(8,128)S(1)} %bitcast.66, f32[896,128]{1,0:T(8,128)S(1)} %bitcast.67, bf16[896,128]{1,0:T(8,128)(2,1)S(1)} %bitcast.60, bf16[896,128]{1,0:T(8,128)(2,1)S(1)} %bitcast.58, ...), custom_call_target="tpu_custom_call" | custom-call | tf_op jit(solution)/shard_map/pallas_call | solution.py:108
  28.4 19.6 %all_to_all.22.in_ref = bf16[8,112,128]{2,1,0:T(8,128)(2,1)S(1)} all-to-all(bf16[8,112,128]{2,1,0:T(8,128)(2,1)S(1)} %bitcast.65), channel_id=1, replica_groups={{256,384,448,0,64,320,192,128},{257,385,449,1,65,321,193,129},{258,386,..., dimensions={0} | all-to-all | bytes 458752 | tf_op jit(solution)/shard_map/all_to_all | solution.py:138
  48.0 0.0 copy-start.3
  48.0 14.4 %all_to_all.23.average_ref = bf16[8,112,128]{2,1,0:T(8,128)(2,1)S(1)} all-to-all(bf16[8,112,128]{2,1,0:T(8,128)(2,1)S(1)} %shard_map.70), channel_id=1, replica_groups={{256,384,64,128,320,192,0,448},{257,385,65,129,321,193,1,449},{258,386,..., dimensions={0} | all-to-all | bytes 458752 | tf_op jit(solution)/shard_map/all_to_all | solution.py:140
  62.4 0.0 copy-done.3
  62.4 1.0 %shard_map.71 = (f32[896,128]{1,0:T(8,128)}, f32[896,128]{1,0:T(8,128)}) custom-call(bf16[8,112,128]{2,1,0:T(8,128)(2,1)S(1)} %all_to_all.23.average_ref, f32[896,128]{1,0:T(8,128)S(1)} %bitcast.64, f32[896,128]{1,0:T(8,128)S(1)} %bitcast.68), custom_call_target="tpu_custom_call" | custom-call | tf_op jit(solution)/shard_map/pallas_call | solution.py:108
  (1 shorter events, 0.0 us)
Async XLA Ops:
  0.6 26.8 %copy-start.2 = (f32[1,4,28672]{2,1,0:T(4,128)S(1)}, f32[1,4,28672]{2,1,0:T(4,128)}, u32[]{:S(2)}) copy-start(f32[1,4,28672]{2,1,0:T(4,128)} %param.8) | copy-start | bytes 1376260
  2.3 25.2 %copy-start = (f32[4,28672]{1,0:T(4,128)S(1)}, f32[4,28672]{1,0:T(4,128)}, u32[]{:S(2)}) copy-start(f32[4,28672]{1,0:T(4,128)} %param.5) | copy-start | bytes 1376260
  2.3 25.2 %copy-start.1 = (f32[1,4,28672]{2,1,0:T(4,128)S(1)}, f32[1,4,28672]{2,1,0:T(4,128)}, u32[]{:S(2)}) copy-start(f32[1,4,28672]{2,1,0:T(4,128)} %param.7) | copy-start | bytes 1376260
  48.0 14.4 %copy-start.3 = (f32[4,28672]{1,0:T(4,128)S(1)}, f32[4,28672]{1,0:T(4,128)}, u32[]{:S(2)}) copy-start(f32[4,28672]{1,0:T(4,128)} %param.6) | copy-start | bytes 1376260

commit v4 on v3

--- a/solution.py
+++ b/solution.py
@@ -16,7 +16,7 @@
 sent = jnp.bfloat16
 
 codes_order = [4, 6, 7, 0, 1, 5, 3, 2]
-means_order = [4, 6, 1, 2, 5, 3, 0, 7]
+means_order = [4, 2, 1, 7, 5, 3, 0, 6]
 totals_first = ((2 * 2 + 1) * 4 + 2) * 2
 totals_order = [totals_first] + [k for k in range(64) if k != totals_first]
 

time: 63.6 us -> 62.5 us (0.983)
  blocking collectives: 58.9 us -> 57.6 us
    all_to_all x1, blocking collectives: 14.4 us -> 13 us  [body(): lax.all_to_all(mean, 'group', 0, 0, tiled=True, axis_index_groups=[means_...]
where the time goes in v4:
time: 62.5 us; the launch traced here: 62.1 us
  blocking collectives  57.6 us (92%)
  Pallas kernels  2.17 us (3%)
  local copies, waits for them, and re-layouts  1.66 us (3%)
  between operations  0.68 us (1%)
    all_to_all x1, blocking collectives, body(): lax.all_to_all(squares, 'fsdp', 0, 0, tiled=True, axis_index_groups=[tota...  25 us
    all_to_all x1, blocking collectives, body(): lax.all_to_all(delta, 'group', 0, 0, tiled=True, axis_index_groups=[codes...  19.6 us
    all_to_all x1, blocking collectives, body(): lax.all_to_all(mean, 'group', 0, 0, tiled=True, axis_index_groups=[means_...  13 us
    pallas_call x4, Pallas kernels, call(): pl.pallas_call(kernel, out_shape=out_shape, compiler_params=pltpu.Compile...  2.17 us
    slice x1, local copies, waits for them, and re-layouts, body(): inner_grads[0, step]  1.64 us

profile of v4, /device:TPU:6, one launch (start us, length us, event | category | flops | bytes accessed | tf_op | source)
XLA Modules:
  0.0 62.1 jit_solution(14682521312056576881)
XLA Ops:
  0.6 0.0 copy-start.2
  0.6 1.6 %fusion = (bf16[1,1,4,28672]{3,2,1,0:T(4,128)(2,1)S(1)}, bf16[1,1,4,28672]{3,2,1,0:T(4,128)(2,1)S(1)}, bf16[1,1,4,28672]{3,2,1,0:T(4,128)(2,1)S(1)}, bf16[1,1,4,28672]{3,2,1,0:T(4,128)(2,1)S(1)}) fusion(bf16[1,4,4,28672]{3,2,1,0:T(4,128)(2,1)} %param.9), kind=kLoop, calls=%fused_computation | loop fusion | bytes 1835008 | tf_op jit(solution)/shard_map/slice | solution.py:124
  2.3 0.0 copy-start
  2.3 0.0 copy-start.1
  2.3 0.2 shard_map.68
  2.5 25.0 %all_to_all.21 = f32[64,1,128]{2,1,0:T(1,128)S(1)} all-to-all(f32[64,1,128]{2,1,0:T(1,128)S(1)} %bitcast.70), channel_id=1, replica_groups={{44,0,1,2,3,4,5,6,7,8,9,10,11,12,13,14,15,16,17,18,19,20,21,22,23,24,25..., dimensions={0} | all-to-all | bytes 65536 | tf_op jit(solution)/shard_map/all_to_all | solution.py:127
  27.4 0.0 copy-done.2
  27.5 0.0 copy-done
  27.5 0.0 copy-done.1
  27.5 0.9 %shard_map.69 = bf16[896,128]{1,0:T(8,128)(2,1)S(1)} custom-call(f32[64,128]{1,0:T(8,128)S(1)} %bitcast.69, f32[896,128]{1,0:T(8,128)S(1)} %bitcast.63, f32[896,128]{1,0:T(8,128)S(1)} %bitcast.66, f32[896,128]{1,0:T(8,128)S(1)} %bitcast.67, bf16[896,128]{1,0:T(8,128)(2,1)S(1)} %bitcast.60, bf16[896,128]{1,0:T(8,128)(2,1)S(1)} %bitcast.58, ...), custom_call_target="tpu_custom_call" | custom-call | tf_op jit(solution)/shard_map/pallas_call | solution.py:108
  28.4 19.6 %all_to_all.22.in_ref = bf16[8,112,128]{2,1,0:T(8,128)(2,1)S(1)} all-to-all(bf16[8,112,128]{2,1,0:T(8,128)(2,1)S(1)} %bitcast.65), channel_id=1, replica_groups={{256,384,448,0,64,320,192,128},{257,385,449,1,65,321,193,129},{258,386,..., dimensions={0} | all-to-all | bytes 458752 | tf_op jit(solution)/shard_map/all_to_all | solution.py:138
  48.0 0.0 copy-start.3
  48.0 13.0 %all_to_all.23.average_ref = bf16[8,112,128]{2,1,0:T(8,128)(2,1)S(1)} all-to-all(bf16[8,112,128]{2,1,0:T(8,128)(2,1)S(1)} %shard_map.70), channel_id=1, replica_groups={{256,128,64,448,320,192,0,384},{257,129,65,449,321,193,1,385},{258,130,..., dimensions={0} | all-to-all | bytes 458752 | tf_op jit(solution)/shard_map/all_to_all | solution.py:140
  61.1 0.0 copy-done.3
  61.1 1.0 %shard_map.71 = (f32[896,128]{1,0:T(8,128)}, f32[896,128]{1,0:T(8,128)}) custom-call(bf16[8,112,128]{2,1,0:T(8,128)(2,1)S(1)} %all_to_all.23.average_ref, f32[896,128]{1,0:T(8,128)S(1)} %bitcast.64, f32[896,128]{1,0:T(8,128)S(1)} %bitcast.68), custom_call_target="tpu_custom_call" | custom-call | tf_op jit(solution)/shard_map/pallas_call | solution.py:108
  (1 shorter events, 0.0 us)
Async XLA Ops:
  0.6 26.8 %copy-start.2 = (f32[1,4,28672]{2,1,0:T(4,128)S(1)}, f32[1,4,28672]{2,1,0:T(4,128)}, u32[]{:S(2)}) copy-start(f32[1,4,28672]{2,1,0:T(4,128)} %param.8) | copy-start | bytes 1376260
  2.3 25.2 %copy-start = (f32[4,28672]{1,0:T(4,128)S(1)}, f32[4,28672]{1,0:T(4,128)}, u32[]{:S(2)}) copy-start(f32[4,28672]{1,0:T(4,128)} %param.5) | copy-start | bytes 1376260
  2.3 25.2 %copy-start.1 = (f32[1,4,28672]{2,1,0:T(4,128)S(1)}, f32[1,4,28672]{2,1,0:T(4,128)}, u32[]{:S(2)}) copy-start(f32[1,4,28672]{2,1,0:T(4,128)} %param.7) | copy-start | bytes 1376260
  48.0 13.1 %copy-start.3 = (f32[4,28672]{1,0:T(4,128)S(1)}, f32[4,28672]{1,0:T(4,128)}, u32[]{:S(2)}) copy-start(f32[4,28672]{1,0:T(4,128)} %param.6) | copy-start | bytes 1376260

commit v5 on v4

--- a/solution.py
+++ b/solution.py
@@ -29,27 +29,39 @@
     return x.reshape(lead + (rows * width // 128, 128))
 
 
+def in_hbm(x):
+    return pltpu.with_memory_space_constraint(x, pltpu.HBM)
+
+
 def from_rows(x, rows, width):
     return jnp.swapaxes(x.reshape(width // 128, rows, 128), 0, 1).reshape(rows, width)
 
 
-def squares_kernel(*refs):
-    grads_refs, out_ref = refs[:-1], refs[-1]
-    steps, (length, _) = len(grads_refs), grads_refs[0].shape
+def squares_kernel(grads_ref, two_ref, out_ref, grads_held_ref, two_held_ref, sems, two_sem):
+    steps, length, _ = grads_ref.shape
+    copies = [
+        pltpu.make_async_copy(grads_ref.at[step], grads_held_ref.at[step], sems.at[step])
+        for step in range(steps)
+    ]
+    two_copy = pltpu.make_async_copy(two_ref, two_held_ref, two_sem)
+    for copy in copies:
+        copy.start()
+    two_copy.start()
     lane = lax.broadcasted_iota(jnp.int32, (1, 128), 1)
     row = jnp.zeros((1, 128), jnp.float32)
     for step in range(steps):
+        copies[step].wait()
         total = jnp.zeros((16, 128), jnp.float32)
         for at in range(0, length, 16):
-            grad = grads_refs[step][at : at + 16, :].astype(jnp.float32)
+            grad = grads_held_ref[step, at : at + 16, :].astype(jnp.float32)
             total = total + grad * grad
         row = jnp.where(lane == step, jnp.sum(total), row)
     out_ref[...] = jnp.broadcast_to(row, out_ref.shape)
+    two_copy.wait()
 
 
-def inner_kernel(totals_ref, params_ref, one_ref, two_ref, *refs):
-    grads_refs, out_ref = refs[:-1], refs[-1]
-    steps, (length, _) = len(grads_refs), grads_refs[0].shape
+def inner_kernel(totals_ref, params_ref, one_ref, two_ref, grads_ref, out_ref):
+    steps, length, _ = grads_ref.shape
     totals = jnp.sum(totals_ref[...], axis=0, keepdims=True)
     factors = jnp.minimum(1.0, clip_norm / (jnp.sqrt(totals) + 1e-06))
     lane = lax.broadcasted_iota(jnp.int32, (1, 128), 1)
@@ -70,7 +82,7 @@
         moment_one = one_ref[rows, :]
         moment_two = two_ref[rows, :]
         for step in range(steps):
-            grad = grads_refs[step][rows, :].astype(jnp.float32)
+            grad = grads_ref[step, rows, :].astype(jnp.float32)
             moment_one = moment_one + adds_one[step] * grad
             moment_two = moment_two + adds_two[step] * (grad * grad)
             root = moment_two * lax.rsqrt(moment_two) + terms[step]
@@ -104,10 +116,12 @@
             )
 
 
-def call(kernel, out_shape, *args):
+def call(kernel, out_shape, *args, space=pltpu.VMEM, scratch=()):
     return pl.pallas_call(
         kernel,
         out_shape=out_shape,
+        in_specs=[pl.BlockSpec(memory_space=space)] * len(args),
+        scratch_shapes=scratch,
         compiler_params=pltpu.CompilerParams(vmem_limit_bytes=16 * 1024 * 1024),
     )(*args)
 
@@ -120,10 +134,21 @@
     params = to_rows(outer_params)
     momentum = to_rows(outer_momentum)
     moment_one = to_rows(first_moment[0])
-    moment_two = to_rows(second_moment[0])
-    grads = [to_rows(inner_grads[0, step]) for step in range(inner_grads.shape[1])]
+    moment_two = in_hbm(to_rows(second_moment[0]))
+    grads = in_hbm(to_rows(inner_grads[0]))
     f32 = jnp.float32
-    squares = call(squares_kernel, jax.ShapeDtypeStruct((shards, 128), f32), *grads)
+    squares, grads, moment_two = call(
+        squares_kernel,
+        (
+            jax.ShapeDtypeStruct((shards, 128), f32),
+            jax.ShapeDtypeStruct(grads.shape, grads.dtype),
+            jax.ShapeDtypeStruct(moment_two.shape, moment_two.dtype),
+        ),
+        grads,
+        moment_two,
+        space=pltpu.HBM,
+        scratch=(pltpu.SemaphoreType.DMA((grads.shape[0],)), pltpu.SemaphoreType.DMA),
+    )
     totals = lax.all_to_all(squares, "fsdp", 0, 0, tiled=True, axis_index_groups=[totals_order])
     delta = call(
         inner_kernel,
@@ -132,7 +157,7 @@
         params,
         moment_one,
         moment_two,
-        *grads,
+        grads,
     )
     delta = delta.reshape(replicas, length // replicas, 128)
     parts = lax.all_to_all(delta, "group", 0, 0, tiled=True, axis_index_groups=[codes_order])

time: 62.5 us -> 62.2 us (level)
  local copies, waits for them, and re-layouts: 1.66 us -> 0.01 us
  Pallas kernels: 2.17 us -> 3.67 us
    slice x1 -> x0, local copies, waits for them, and re-layouts: 1.64 us -> none  [body(): inner_grads[0, step]]
    pallas_call x4, Pallas kernels: 2.17 us -> 3.67 us  [call(): pl.pallas_call(kernel, out_shape=out_shape, in_specs=[pl.BlockSpec(memory...]
where the time goes in v5:
time: 62.2 us; the launch traced here: 61.8 us
  blocking collectives  57.4 us (92%)
  Pallas kernels  3.67 us (6%)
  between operations  0.67 us (1%)
    all_to_all x1, blocking collectives, body(): lax.all_to_all(squares, 'fsdp', 0, 0, tiled=True, axis_index_groups=[tota...  24.8 us
    all_to_all x1, blocking collectives, body(): lax.all_to_all(delta, 'group', 0, 0, tiled=True, axis_index_groups=[codes...  19.6 us
    all_to_all x1, blocking collectives, body(): lax.all_to_all(mean, 'group', 0, 0, tiled=True, axis_index_groups=[means_...  13 us
    pallas_call x4, Pallas kernels, call(): pl.pallas_call(kernel, out_shape=out_shape, in_specs=[pl.BlockSpec(memory...  3.67 us

profile of v5, /device:TPU:6, one launch (start us, length us, event | category | flops | bytes accessed | tf_op | source)
XLA Modules:
  0.0 61.8 jit_solution(13743344100529442131)
XLA Ops:
  0.6 0.0 copy-start
  0.6 0.0 copy-start.1
  0.7 1.7 %shard_map.68 = (f32[64,128]{1,0:T(8,128)S(1)}, bf16[4,896,128]{2,1,0:T(8,128)(2,1)S(1)}, f32[896,128]{1,0:T(8,128)S(1)}) custom-call(bf16[4,896,128]{2,1,0:T(8,128)(2,1)} %bitcast.47, f32[896,128]{1,0:T(8,128)} %bitcast.48), custom_call_target="tpu_custom_call" | custom-call | tf_op jit(solution)/shard_map/pallas_call | solution.py:120
  2.3 24.8 %all_to_all.21 = f32[64,1,128]{2,1,0:T(1,128)S(1)} all-to-all(f32[64,1,128]{2,1,0:T(1,128)S(1)} %bitcast.46), channel_id=1, replica_groups={{44,0,1,2,3,4,5,6,7,8,9,10,11,12,13,14,15,16,17,18,19,20,21,22,23,24,25..., dimensions={0} | all-to-all | bytes 65536 | tf_op jit(solution)/shard_map/all_to_all | solution.py:152
  27.2 0.0 copy-done
  27.2 0.0 copy-done.1
  27.2 0.9 %shard_map.69 = bf16[896,128]{1,0:T(8,128)(2,1)S(1)} custom-call(f32[64,128]{1,0:T(8,128)S(1)} %bitcast.45, f32[896,128]{1,0:T(8,128)S(1)} %bitcast.40, f32[896,128]{1,0:T(8,128)S(1)} %bitcast.43, f32[896,128]{1,0:T(8,128)S(1)} %get-tuple-element.8.two_ref, bf16[4,896,128]{2,1,0:T(8,128)(2,1)S(1)} %get-tuple-element.9.grads_ref), custom_call_target="tpu_custom_call" | custom-call | tf_op jit(solution)/shard_map/pallas_call | solution.py:120
  28.1 19.6 %all_to_all.22.in_ref = bf16[8,112,128]{2,1,0:T(8,128)(2,1)S(1)} all-to-all(bf16[8,112,128]{2,1,0:T(8,128)(2,1)S(1)} %bitcast.42), channel_id=1, replica_groups={{256,384,448,0,64,320,192,128},{257,385,449,1,65,321,193,129},{258,386,..., dimensions={0} | all-to-all | bytes 458752 | tf_op jit(solution)/shard_map/all_to_all | solution.py:163
  47.7 0.0 copy-start.2
  47.7 13.0 %all_to_all.23.average_ref = bf16[8,112,128]{2,1,0:T(8,128)(2,1)S(1)} all-to-all(bf16[8,112,128]{2,1,0:T(8,128)(2,1)S(1)} %shard_map.70), channel_id=1, replica_groups={{256,128,64,448,320,192,0,384},{257,129,65,449,321,193,1,385},{258,130,..., dimensions={0} | all-to-all | bytes 458752 | tf_op jit(solution)/shard_map/all_to_all | solution.py:165
  60.8 0.0 copy-done.2
  60.8 1.0 %shard_map.71 = (f32[896,128]{1,0:T(8,128)}, f32[896,128]{1,0:T(8,128)}) custom-call(bf16[8,112,128]{2,1,0:T(8,128)(2,1)S(1)} %all_to_all.23.average_ref, f32[896,128]{1,0:T(8,128)S(1)} %bitcast.41, f32[896,128]{1,0:T(8,128)S(1)} %bitcast.44), custom_call_target="tpu_custom_call" | custom-call | tf_op jit(solution)/shard_map/pallas_call | solution.py:120
  (1 shorter events, 0.0 us)
Async XLA Ops:
  0.6 26.5 %copy-start = (f32[4,28672]{1,0:T(4,128)S(1)}, f32[4,28672]{1,0:T(4,128)}, u32[]{:S(2)}) copy-start(f32[4,28672]{1,0:T(4,128)} %param.5) | copy-start | bytes 1376260
  0.6 26.5 %copy-start.1 = (f32[1,4,28672]{2,1,0:T(4,128)S(1)}, f32[1,4,28672]{2,1,0:T(4,128)}, u32[]{:S(2)}) copy-start(f32[1,4,28672]{2,1,0:T(4,128)} %param.7) | copy-start | bytes 1376260
  47.7 13.1 %copy-start.2 = (f32[4,28672]{1,0:T(4,128)S(1)}, f32[4,28672]{1,0:T(4,128)}, u32[]{:S(2)}) copy-start(f32[4,28672]{1,0:T(4,128)} %param.6) | copy-start | bytes 1376260

commit v6 on v5

--- a/solution.py
+++ b/solution.py
@@ -17,7 +17,7 @@
 
 codes_order = [4, 6, 7, 0, 1, 5, 3, 2]
 means_order = [4, 2, 1, 7, 5, 3, 0, 6]
-totals_first = ((2 * 2 + 1) * 4 + 2) * 2
+totals_first = ((2 * 2 + 1) * 4 + 2) * 2 + 1
 totals_order = [totals_first] + [k for k in range(64) if k != totals_first]
 
 

time: 62.2 us -> 61.9 us (level)
  no operation moved by 1% of the time
where the time goes in v6:
time: 61.9 us; the launch traced here: 61.5 us
  blocking collectives  57.2 us (92%)
  Pallas kernels  3.67 us (6%)
  between operations  0.67 us (1%)
    all_to_all x1, blocking collectives, body(): lax.all_to_all(squares, 'fsdp', 0, 0, tiled=True, axis_index_groups=[tota...  24.6 us
    all_to_all x1, blocking collectives, body(): lax.all_to_all(delta, 'group', 0, 0, tiled=True, axis_index_groups=[codes...  19.6 us
    all_to_all x1, blocking collectives, body(): lax.all_to_all(mean, 'group', 0, 0, tiled=True, axis_index_groups=[means_...  13 us
    pallas_call x4, Pallas kernels, call(): pl.pallas_call(kernel, out_shape=out_shape, in_specs=[pl.BlockSpec(memory...  3.67 us

profile of v6, /device:TPU:6, one launch (start us, length us, event | category | flops | bytes accessed | tf_op | source)
XLA Modules:
  0.0 61.5 jit_solution(2671927405549020615)
XLA Ops:
  0.6 0.0 copy-start
  0.6 0.0 copy-start.1
  0.7 1.7 %shard_map.68 = (f32[64,128]{1,0:T(8,128)S(1)}, bf16[4,896,128]{2,1,0:T(8,128)(2,1)S(1)}, f32[896,128]{1,0:T(8,128)S(1)}) custom-call(bf16[4,896,128]{2,1,0:T(8,128)(2,1)} %bitcast.47, f32[896,128]{1,0:T(8,128)} %bitcast.48), custom_call_target="tpu_custom_call" | custom-call | tf_op jit(solution)/shard_map/pallas_call | solution.py:120
  2.3 24.6 %all_to_all.21 = f32[64,1,128]{2,1,0:T(1,128)S(1)} all-to-all(f32[64,1,128]{2,1,0:T(1,128)S(1)} %bitcast.46), channel_id=1, replica_groups={{45,0,1,2,3,4,5,6,7,8,9,10,11,12,13,14,15,16,17,18,19,20,21,22,23,24,25..., dimensions={0} | all-to-all | bytes 65536 | tf_op jit(solution)/shard_map/all_to_all | solution.py:152
  26.9 0.0 copy-done
  26.9 0.0 copy-done.1
  26.9 0.9 %shard_map.69 = bf16[896,128]{1,0:T(8,128)(2,1)S(1)} custom-call(f32[64,128]{1,0:T(8,128)S(1)} %bitcast.45, f32[896,128]{1,0:T(8,128)S(1)} %bitcast.40, f32[896,128]{1,0:T(8,128)S(1)} %bitcast.43, f32[896,128]{1,0:T(8,128)S(1)} %get-tuple-element.8.two_ref, bf16[4,896,128]{2,1,0:T(8,128)(2,1)S(1)} %get-tuple-element.9.grads_ref), custom_call_target="tpu_custom_call" | custom-call | tf_op jit(solution)/shard_map/pallas_call | solution.py:120
  27.8 19.6 %all_to_all.22.in_ref = bf16[8,112,128]{2,1,0:T(8,128)(2,1)S(1)} all-to-all(bf16[8,112,128]{2,1,0:T(8,128)(2,1)S(1)} %bitcast.42), channel_id=1, replica_groups={{256,384,448,0,64,320,192,128},{257,385,449,1,65,321,193,129},{258,386,..., dimensions={0} | all-to-all | bytes 458752 | tf_op jit(solution)/shard_map/all_to_all | solution.py:163
  47.4 0.0 copy-start.2
  47.4 13.0 %all_to_all.23.average_ref = bf16[8,112,128]{2,1,0:T(8,128)(2,1)S(1)} all-to-all(bf16[8,112,128]{2,1,0:T(8,128)(2,1)S(1)} %shard_map.70), channel_id=1, replica_groups={{256,128,64,448,320,192,0,384},{257,129,65,449,321,193,1,385},{258,130,..., dimensions={0} | all-to-all | bytes 458752 | tf_op jit(solution)/shard_map/all_to_all | solution.py:165
  60.5 0.0 copy-done.2
  60.5 1.0 %shard_map.71 = (f32[896,128]{1,0:T(8,128)}, f32[896,128]{1,0:T(8,128)}) custom-call(bf16[8,112,128]{2,1,0:T(8,128)(2,1)S(1)} %all_to_all.23.average_ref, f32[896,128]{1,0:T(8,128)S(1)} %bitcast.41, f32[896,128]{1,0:T(8,128)S(1)} %bitcast.44), custom_call_target="tpu_custom_call" | custom-call | tf_op jit(solution)/shard_map/pallas_call | solution.py:120
  (1 shorter events, 0.0 us)
Async XLA Ops:
  0.6 26.3 %copy-start = (f32[4,28672]{1,0:T(4,128)S(1)}, f32[4,28672]{1,0:T(4,128)}, u32[]{:S(2)}) copy-start(f32[4,28672]{1,0:T(4,128)} %param.5) | copy-start | bytes 1376260
  0.6 26.2 %copy-start.1 = (f32[1,4,28672]{2,1,0:T(4,128)S(1)}, f32[1,4,28672]{2,1,0:T(4,128)}, u32[]{:S(2)}) copy-start(f32[1,4,28672]{2,1,0:T(4,128)} %param.7) | copy-start | bytes 1376260
  47.4 13.1 %copy-start.2 = (f32[4,28672]{1,0:T(4,128)S(1)}, f32[4,28672]{1,0:T(4,128)}, u32[]{:S(2)}) copy-start(f32[4,28672]{1,0:T(4,128)} %param.6) | copy-start | bytes 1376260

commit v7 on v6

--- a/solution.py
+++ b/solution.py
@@ -55,7 +55,8 @@
         for at in range(0, length, 16):
             grad = grads_held_ref[step, at : at + 16, :].astype(jnp.float32)
             total = total + grad * grad
-        row = jnp.where(lane == step, jnp.sum(total), row)
+        total = jnp.sum(jnp.sum(total, axis=0, keepdims=True), axis=1, keepdims=True)
+        row = jnp.where(lane == step, total, row)
     out_ref[...] = jnp.broadcast_to(row, out_ref.shape)
     two_copy.wait()
 
@@ -68,7 +69,8 @@
     kept = (1.0 - inner_rate * decay_rate) ** steps
     adds_one, adds_two, terms, weights = [], [], [], []
     for step in range(steps):
-        factor = jnp.sum(jnp.where(lane == step, factors, 0.0))
+        factor = jnp.sum(jnp.where(lane == step, factors, 0.0), axis=1, keepdims=True)
+        factor = jnp.broadcast_to(factor, (16, 128))
         shrunk_one = beta_one ** (step + 1)
         shrunk_two = beta_two ** (step + 1)
         left = (1.0 - inner_rate * decay_rate) ** (steps - 1 - step)

time: 61.9 us -> 61.9 us (level)
  no operation moved by 1% of the time
where the time goes in v7:
time: 61.9 us; the launch traced here: 61.4 us
  blocking collectives  57.2 us (92%)
  Pallas kernels  3.61 us (6%)
  between operations  0.67 us (1%)
    all_to_all x1, blocking collectives, body(): lax.all_to_all(squares, 'fsdp', 0, 0, tiled=True, axis_index_groups=[tota...  24.6 us
    all_to_all x1, blocking collectives, body(): lax.all_to_all(delta, 'group', 0, 0, tiled=True, axis_index_groups=[codes...  19.6 us
    all_to_all x1, blocking collectives, body(): lax.all_to_all(mean, 'group', 0, 0, tiled=True, axis_index_groups=[means_...  13 us
    pallas_call x4, Pallas kernels, call(): pl.pallas_call(kernel, out_shape=out_shape, in_specs=[pl.BlockSpec(memory...  3.61 us

profile of v7, /device:TPU:6, one launch (start us, length us, event | category | flops | bytes accessed | tf_op | source)
XLA Modules:
  0.0 61.4 jit_solution(7302893896403133024)
XLA Ops:
  0.6 0.0 copy-start
  0.6 0.0 copy-start.1
  0.7 1.5 %shard_map.68 = (f32[64,128]{1,0:T(8,128)S(1)}, bf16[4,896,128]{2,1,0:T(8,128)(2,1)S(1)}, f32[896,128]{1,0:T(8,128)S(1)}) custom-call(bf16[4,896,128]{2,1,0:T(8,128)(2,1)} %bitcast.47, f32[896,128]{1,0:T(8,128)} %bitcast.48), custom_call_target="tpu_custom_call" | custom-call | tf_op jit(solution)/shard_map/pallas_call | solution.py:122
  2.2 24.6 %all_to_all.21 = f32[64,1,128]{2,1,0:T(1,128)S(1)} all-to-all(f32[64,1,128]{2,1,0:T(1,128)S(1)} %bitcast.46), channel_id=1, replica_groups={{45,0,1,2,3,4,5,6,7,8,9,10,11,12,13,14,15,16,17,18,19,20,21,22,23,24,25..., dimensions={0} | all-to-all | bytes 65536 | tf_op jit(solution)/shard_map/all_to_all | solution.py:154
  26.8 0.0 copy-done
  26.8 0.0 copy-done.1
  26.8 1.0 %shard_map.69 = bf16[896,128]{1,0:T(8,128)(2,1)S(1)} custom-call(f32[64,128]{1,0:T(8,128)S(1)} %bitcast.45, f32[896,128]{1,0:T(8,128)S(1)} %bitcast.40, f32[896,128]{1,0:T(8,128)S(1)} %bitcast.43, f32[896,128]{1,0:T(8,128)S(1)} %get-tuple-element.8.two_ref, bf16[4,896,128]{2,1,0:T(8,128)(2,1)S(1)} %get-tuple-element.9.grads_ref), custom_call_target="tpu_custom_call" | custom-call | tf_op jit(solution)/shard_map/pallas_call | solution.py:122
  27.8 19.6 %all_to_all.22.in_ref = bf16[8,112,128]{2,1,0:T(8,128)(2,1)S(1)} all-to-all(bf16[8,112,128]{2,1,0:T(8,128)(2,1)S(1)} %bitcast.42), channel_id=1, replica_groups={{256,384,448,0,64,320,192,128},{257,385,449,1,65,321,193,129},{258,386,..., dimensions={0} | all-to-all | bytes 458752 | tf_op jit(solution)/shard_map/all_to_all | solution.py:165
  47.3 0.0 copy-start.2
  47.4 13.0 %all_to_all.23.average_ref = bf16[8,112,128]{2,1,0:T(8,128)(2,1)S(1)} all-to-all(bf16[8,112,128]{2,1,0:T(8,128)(2,1)S(1)} %shard_map.70), channel_id=1, replica_groups={{256,128,64,448,320,192,0,384},{257,129,65,449,321,193,1,385},{258,130,..., dimensions={0} | all-to-all | bytes 458752 | tf_op jit(solution)/shard_map/all_to_all | solution.py:167
  60.4 0.0 copy-done.2
  60.4 1.0 %shard_map.71 = (f32[896,128]{1,0:T(8,128)}, f32[896,128]{1,0:T(8,128)}) custom-call(bf16[8,112,128]{2,1,0:T(8,128)(2,1)S(1)} %all_to_all.23.average_ref, f32[896,128]{1,0:T(8,128)S(1)} %bitcast.41, f32[896,128]{1,0:T(8,128)S(1)} %bitcast.44), custom_call_target="tpu_custom_call" | custom-call | tf_op jit(solution)/shard_map/pallas_call | solution.py:122
  (1 shorter events, 0.0 us)
Async XLA Ops:
  0.6 26.1 %copy-start = (f32[4,28672]{1,0:T(4,128)S(1)}, f32[4,28672]{1,0:T(4,128)}, u32[]{:S(2)}) copy-start(f32[4,28672]{1,0:T(4,128)} %param.5) | copy-start | bytes 1376260
  0.6 26.1 %copy-start.1 = (f32[1,4,28672]{2,1,0:T(4,128)S(1)}, f32[1,4,28672]{2,1,0:T(4,128)}, u32[]{:S(2)}) copy-start(f32[1,4,28672]{2,1,0:T(4,128)} %param.7) | copy-start | bytes 1376260
  47.3 13.1 %copy-start.2 = (f32[4,28672]{1,0:T(4,128)S(1)}, f32[4,28672]{1,0:T(4,128)}, u32[]{:S(2)}) copy-start(f32[4,28672]{1,0:T(4,128)} %param.6) | copy-start | bytes 1376260

commit v8 on v7

--- a/solution.py
+++ b/solution.py
@@ -69,8 +69,7 @@
     kept = (1.0 - inner_rate * decay_rate) ** steps
     adds_one, adds_two, terms, weights = [], [], [], []
     for step in range(steps):
-        factor = jnp.sum(jnp.where(lane == step, factors, 0.0), axis=1, keepdims=True)
-        factor = jnp.broadcast_to(factor, (16, 128))
+        factor = jnp.sum(jnp.where(lane == step, factors, 0.0))
         shrunk_one = beta_one ** (step + 1)
         shrunk_two = beta_two ** (step + 1)
         left = (1.0 - inner_rate * decay_rate) ** (steps - 1 - step)

time: 61.9 us -> 61.8 us (level)
  no operation moved by 1% of the time
where the time goes in v8:
time: 61.8 us; the launch traced here: 61.4 us
  blocking collectives  57.2 us (93%)
  Pallas kernels  3.54 us (6%)
  between operations  0.67 us (1%)
    all_to_all x1, blocking collectives, body(): lax.all_to_all(squares, 'fsdp', 0, 0, tiled=True, axis_index_groups=[tota...  24.6 us
    all_to_all x1, blocking collectives, body(): lax.all_to_all(delta, 'group', 0, 0, tiled=True, axis_index_groups=[codes...  19.6 us
    all_to_all x1, blocking collectives, body(): lax.all_to_all(mean, 'group', 0, 0, tiled=True, axis_index_groups=[means_...  13 us
    pallas_call x4, Pallas kernels, call(): pl.pallas_call(kernel, out_shape=out_shape, in_specs=[pl.BlockSpec(memory...  3.54 us

profile of v8, /device:TPU:6, one launch (start us, length us, event | category | flops | bytes accessed | tf_op | source)
XLA Modules:
  0.0 61.4 jit_solution(15696844253629944318)
XLA Ops:
  0.6 0.0 copy-start
  0.6 0.0 copy-start.1
  0.7 1.5 %shard_map.68 = (f32[64,128]{1,0:T(8,128)S(1)}, bf16[4,896,128]{2,1,0:T(8,128)(2,1)S(1)}, f32[896,128]{1,0:T(8,128)S(1)}) custom-call(bf16[4,896,128]{2,1,0:T(8,128)(2,1)} %bitcast.47, f32[896,128]{1,0:T(8,128)} %bitcast.48), custom_call_target="tpu_custom_call" | custom-call | tf_op jit(solution)/shard_map/pallas_call | solution.py:121
  2.2 24.6 %all_to_all.21 = f32[64,1,128]{2,1,0:T(1,128)S(1)} all-to-all(f32[64,1,128]{2,1,0:T(1,128)S(1)} %bitcast.46), channel_id=1, replica_groups={{45,0,1,2,3,4,5,6,7,8,9,10,11,12,13,14,15,16,17,18,19,20,21,22,23,24,25..., dimensions={0} | all-to-all | bytes 65536 | tf_op jit(solution)/shard_map/all_to_all | solution.py:153
  26.8 0.0 copy-done
  26.8 0.0 copy-done.1
  26.8 0.9 %shard_map.69 = bf16[896,128]{1,0:T(8,128)(2,1)S(1)} custom-call(f32[64,128]{1,0:T(8,128)S(1)} %bitcast.45, f32[896,128]{1,0:T(8,128)S(1)} %bitcast.40, f32[896,128]{1,0:T(8,128)S(1)} %bitcast.43, f32[896,128]{1,0:T(8,128)S(1)} %get-tuple-element.8.two_ref, bf16[4,896,128]{2,1,0:T(8,128)(2,1)S(1)} %get-tuple-element.9.grads_ref), custom_call_target="tpu_custom_call" | custom-call | tf_op jit(solution)/shard_map/pallas_call | solution.py:121
  27.7 19.6 %all_to_all.22.in_ref = bf16[8,112,128]{2,1,0:T(8,128)(2,1)S(1)} all-to-all(bf16[8,112,128]{2,1,0:T(8,128)(2,1)S(1)} %bitcast.42), channel_id=1, replica_groups={{256,384,448,0,64,320,192,128},{257,385,449,1,65,321,193,129},{258,386,..., dimensions={0} | all-to-all | bytes 458752 | tf_op jit(solution)/shard_map/all_to_all | solution.py:164
  47.3 0.0 copy-start.2
  47.3 13.0 %all_to_all.23.average_ref = bf16[8,112,128]{2,1,0:T(8,128)(2,1)S(1)} all-to-all(bf16[8,112,128]{2,1,0:T(8,128)(2,1)S(1)} %shard_map.70), channel_id=1, replica_groups={{256,128,64,448,320,192,0,384},{257,129,65,449,321,193,1,385},{258,130,..., dimensions={0} | all-to-all | bytes 458752 | tf_op jit(solution)/shard_map/all_to_all | solution.py:166
  60.3 0.0 copy-done.2
  60.4 1.0 %shard_map.71 = (f32[896,128]{1,0:T(8,128)}, f32[896,128]{1,0:T(8,128)}) custom-call(bf16[8,112,128]{2,1,0:T(8,128)(2,1)S(1)} %all_to_all.23.average_ref, f32[896,128]{1,0:T(8,128)S(1)} %bitcast.41, f32[896,128]{1,0:T(8,128)S(1)} %bitcast.44), custom_call_target="tpu_custom_call" | custom-call | tf_op jit(solution)/shard_map/pallas_call | solution.py:121
  (1 shorter events, 0.0 us)
Async XLA Ops:
  0.6 26.1 %copy-start = (f32[4,28672]{1,0:T(4,128)S(1)}, f32[4,28672]{1,0:T(4,128)}, u32[]{:S(2)}) copy-start(f32[4,28672]{1,0:T(4,128)} %param.5) | copy-start | bytes 1376260
  0.6 26.1 %copy-start.1 = (f32[1,4,28672]{2,1,0:T(4,128)S(1)}, f32[1,4,28672]{2,1,0:T(4,128)}, u32[]{:S(2)}) copy-start(f32[1,4,28672]{2,1,0:T(4,128)} %param.7) | copy-start | bytes 1376260
  47.3 13.1 %copy-start.2 = (f32[4,28672]{1,0:T(4,128)S(1)}, f32[4,28672]{1,0:T(4,128)}, u32[]{:S(2)}) copy-start(f32[4,28672]{1,0:T(4,128)} %param.6) | copy-start | bytes 1376260
